TPU v7x, 512 devices: a whole 4x8x8 slice. The times are simulated.
512 devices in a mesh: half: 2 (over x_lo), grid: 8 (over y), dom: 32 (over z, x_hi, core).
Axes of the slice: x: 4 (x_hi: 2, x_lo: 2; x = x_hi * 2 + x_lo), y: 8, z: 8, core: 2. Of those that a mesh axis runs over, the one named last changes fastest.
Arguments:
- grids: float32 [16, 64, 64, 4096], P(('half', 'grid'), 'dom'), may hold values from -0.8 to 0.8
- levels: int32 [16, 4], replicated, may hold values from 4 to 6, as said below
Outputs:
- combined: float32 [16, 64, 64, 4096], P(('half', 'grid'), 'dom')
Inputs may be any that keep to these rules, and one draw needn't show every extreme that they name: `levels`: with base b = (4, 5, 5, 5), rows 0 to 7 are b plus, in some order, (2,1,1,0), (2,1,0,1), (2,0,1,1), (1,1,1,1), (1,1,0,0), (1,0,1,0), (1,0,0,1), (0,0,0,0); rows 8 to 15 are b plus, in some order, (2,1,0,0), (2,0,1,0), (2,0,0,1), (1,1,1,0), (1,1,0,1), (1,0,1,1), (2,0,0,0), (1,0,0,0).
All inputs are finite; a program needn't handle non-finite values.
Results may differ from a plain program's by a relative error of at most 0.0003.
Values sent between devices are 32-bit elements; how exact they have to be, the bound alone decides.
A program may use at most 128 MiB of HBM per device.

v0:
```python
import jax
import jax.numpy as jnp
import numpy as np
from jax import lax
from jax.sharding import PartitionSpec as P

LEV1 = 6
LEV2 = 6
LEV3 = 6
LEV4 = 6
N1 = 64
N2 = 64
N3 = 64
N4 = 64
HIGH = lax.Precision.HIGHEST
SPANS = (2, 1, 1, 1)


def level_ordering(level):
    points = 2**level
    ordering = [0]
    for section in range(1, level + 1):
        stride = 2 ** (level - section)
        ordering.extend(range(stride, points, 2 * stride))
    return np.array(ordering)


def hier_tables(level_top, spread):
    size_top = 2**level_top
    forwards = np.zeros((spread + 1, size_top, size_top))
    backwards = np.zeros((spread + 1, size_top, size_top))
    for offset in range(spread + 1):
        level = level_top - spread + offset
        points = 2**level
        down_rows = np.eye(points)
        up_rows = np.eye(points)
        for section in range(level, 0, -1):
            stride = 2 ** (level - section)
            odd_points = np.arange(stride, points, 2 * stride)
            down_rows[odd_points] = down_rows[odd_points] - 0.5 * (
                down_rows[odd_points - stride] + down_rows[(odd_points + stride) % points]
            )
        for section in range(1, level + 1):
            stride = 2 ** (level - section)
            odd_points = np.arange(stride, points, 2 * stride)
            up_rows[odd_points] = up_rows[odd_points] + 0.5 * (
                up_rows[odd_points - stride] + up_rows[(odd_points + stride) % points]
            )
        ordering = level_ordering(level)
        forwards[offset, :points, :points] = down_rows[ordering]
        backwards[offset, :points, :points] = up_rows[:, ordering]
    return (jnp.asarray(forwards, jnp.float32), jnp.asarray(backwards, jnp.float32))


def combination_weights(levels):
    corners = np.array(
        [[corner >> place & 1 for place in range(4)] for corner in range(16)], dtype=np.int32
    )
    parity = 1 - 2 * (corners.sum(axis=1) % 2)
    raised = levels[:, None, :] + jnp.asarray(corners, dtype=jnp.int32)[None, :, :]
    below = jnp.all(raised[:, :, None, :] <= levels[None, None, :, :], axis=3)
    inside = jnp.any(below, axis=2).astype(jnp.int32)
    return jnp.sum(inside * jnp.asarray(parity, dtype=jnp.int32)[None, :], axis=1)


def pick_tables(tables, level_column, level_top, spread):
    shifted = level_column - (level_top - spread)
    onehot = (jnp.arange(spread + 1, dtype=jnp.int32)[None, :] == shifted[:, None]).astype(
        jnp.float32
    )
    return jnp.einsum("gs,sij->gij", onehot, tables, precision=HIGH)


def block_cover(levels, upper_block):
    lowest = jnp.array([LEV1 - 2, LEV2 - 1, LEV3 - 1, LEV4 - 1], dtype=jnp.int32)
    offsets = levels - lowest[None, :]
    blocks = jnp.arange(16, dtype=jnp.int32)
    first_block = jnp.minimum(blocks // 4, 2)
    third_block = blocks // 2 % 2
    fourth_block = blocks % 2
    covered = first_block[None, :] <= offsets[:, 0:1]
    covered = covered & (upper_block <= offsets[:, 1:2])
    covered = covered & (third_block[None, :] <= offsets[:, 2:3])
    return covered & (fourth_block[None, :] <= offsets[:, 3:4])


def compact_order(mask):
    ranking = jnp.argsort(jnp.where(mask, 0, 16) + jnp.arange(16, dtype=jnp.int32))
    return (ranking, mask[ranking].astype(jnp.float32))


def pick_rows(blocks, order, valid):
    return jnp.take(blocks, order, axis=0) * valid[:, None]


def place_rows(rows, order, valid):
    return jnp.zeros((16, rows.shape[1]), jnp.float32).at[order].add(rows * valid[:, None])


def combine(blocks, covered):
    order, valid = compact_order(jnp.any(covered, axis=0))
    summed = lax.psum(pick_rows(blocks, order, valid), ("half", "grid"))
    return place_rows(summed, order, valid)


def per_device(grids, levels):
    finest = (LEV1, LEV2, LEV3, LEV4)
    local_count = grids.shape[0]
    rows_here = grids.shape[1]
    grid_count = lax.axis_size("grid")
    group = lax.axis_index("half") * grid_count + lax.axis_index("grid")
    weights = combination_weights(levels).astype(jnp.float32)
    own_levels = lax.dynamic_slice_in_dim(levels, group * local_count, local_count, 0)
    own_weights = lax.dynamic_slice_in_dim(weights, group * local_count, local_count, 0)
    forward_mats = []
    backward_mats = []
    for axis_index in range(4):
        down_tables, up_tables = hier_tables(finest[axis_index], SPANS[axis_index])
        forward_mats.append(
            pick_tables(
                down_tables, own_levels[:, axis_index], finest[axis_index], SPANS[axis_index]
            )
        )
        backward_mats.append(
            pick_tables(up_tables, own_levels[:, axis_index], finest[axis_index], SPANS[axis_index])
        )
    values = grids.reshape(local_count, rows_here, N2, N3, N4)
    values = jnp.einsum("gjl,gabcl->gabcj", forward_mats[3], values, precision=HIGH)
    values = jnp.einsum("gjc,gabcl->gabjl", forward_mats[2], values, precision=HIGH)
    values = jnp.einsum(
        "gjb,gabm->gajm",
        forward_mats[1],
        values.reshape(local_count, rows_here, N2, N3 * N4),
        precision=HIGH,
    )
    surplus = jnp.einsum(
        "gja,gabm->gjbm",
        forward_mats[0],
        lax.all_to_all(values, "dom", split_axis=2, concat_axis=1, tiled=True),
        precision=HIGH,
    )
    scaled = jnp.einsum("g,gjbm->jbm", own_weights, surplus, precision=HIGH)
    pole_rows = scaled.shape[1]
    upper_block = lax.axis_index("dom") * pole_rows // (N2 // 2)
    covered = block_cover(levels, upper_block)
    quarter_rows = N1 // 4
    blocks = (
        scaled.reshape(4, quarter_rows, pole_rows, 2, N3 // 2, 2, N4 // 2)
        .transpose(0, 3, 5, 1, 2, 4, 6)
        .reshape(16, -1)
    )
    summed_blocks = combine(blocks, covered)
    totals = (
        summed_blocks.reshape(4, 2, 2, quarter_rows, pole_rows, N3 // 2, N4 // 2)
        .transpose(0, 3, 4, 1, 5, 2, 6)
        .reshape(N1, pole_rows, N3 * N4)
    )
    expanded = jnp.einsum("gja,abm->gjbm", backward_mats[0], totals, precision=HIGH)
    returned = lax.all_to_all(expanded, "dom", split_axis=1, concat_axis=2, tiled=True)
    returned = jnp.einsum("gjb,gabm->gajm", backward_mats[1], returned, precision=HIGH)
    returned = returned.reshape(local_count, rows_here, N2, N3, N4)
    returned = jnp.einsum("gjc,gabcl->gabjl", backward_mats[2], returned, precision=HIGH)
    returned = jnp.einsum("gjl,gabcl->gabcj", backward_mats[3], returned, precision=HIGH)
    return returned.reshape(local_count, rows_here, N2, N3 * N4)


def solution(mesh):
    return jax.shard_map(
        per_device,
        mesh=mesh,
        in_specs=(P(("half", "grid"), "dom", None, None), P()),
        out_specs=P(("half", "grid"), "dom", None, None),
        check_vma=False,
    )
```

profile of v0, /device:TPU:1, one launch (start us, length us, event | category | flops | bytes accessed | tf_op | source)
XLA Modules:
  0.0 454.5 jit_solution(10062554610760000204)
XLA Ops:
  7.8 4.6 %reshape.191 = f32[2,64,64,64]{3,2,1,0:T(8,128)} reshape(f32[1,2,64,4096]{3,2,1,0:T(8,128)} %param.13) | data formatting | bytes 4194304 | tf_op jit(solution)/shard_map/reshape.17
  14.2 13.8 %fusion.28 = f32[64,2,64,64]{3,0,2,1:T(8,128)S(1)} fusion(f32[64,64,1,1]{1,0,3,2:T(8,128)S(1)} %bitcast.162, f32[2,64,64,64]{3,2,1,0:T(8,128)} %reshape.191), kind=kOutput, calls=%fused_computation.65 | convolution fusion | flops 402653184 | bytes 4210688 | tf_op jit(solution)/shard_map/gjl,gabcl->gabcj/dot_general | solution.py:128
  28.0 4.9 %fusion.4 = f32[1,2,64,64,64]{3,4,2,1,0:T(8,128)} fusion(f32[64,64,1,1]{1,0,3,2:T(8,128)S(1)} %bitcast.161, f32[64,2,64,64]{3,0,2,1:T(8,128)S(1)} %fusion.28), kind=kOutput, calls=%fused_computation.11 | convolution fusion | flops 402653184 | bytes 4210688 | tf_op jit(solution)/shard_map/gjc,gabcl->gabjl/dot_general | solution.py:129
  33.0 5.7 %copy.51 = f32[1,2,64,64,64]{4,3,2,1,0:T(8,128)} copy(f32[1,2,64,64,64]{3,4,2,1,0:T(8,128)} %fusion.4) | data formatting | bytes 4194304 | tf_op jit(solution)/shard_map/gjc,gabcl->gabjl/transpose | solution.py:129
  38.6 3.7 reshape.192
  48.3 14.6 %all-to-all-start = ((f32[1,2,64,4096]{3,1,0,2:T(2,128)}), f32[1,2,64,4096]{3,1,0,2:T(2,128)S(1)}, u32[]{:S(2)}, u32[]{:S(2)}) async-start(f32[1,2,64,4096]{3,1,0,2:T(2,128)} %copy.52), calls=%async_computation | async-start | bytes 4194304 | tf_op jit(solution)/shard_map/all_to_all | solution.py:139
  67.4 45.5 %all-to-all-done = f32[1,2,64,4096]{3,1,0,2:T(2,128)S(1)} async-done(((f32[1,2,64,4096]{3,1,0,2:T(2,128)}), f32[1,2,64,4096]{3,1,0,2:T(2,128)S(1)}, u32[]{:S(2)}, u32[]{:S(2)}) %all-to-all-start) | async-done | bytes 2097184 | tf_op jit(solution)/shard_map/all_to_all | solution.py:139
  114.2 3.3 copy.53
  117.5 3.6 copy.54
  121.1 22.9 %multiply_bitcast_fusion = f32[4,2,2,16,2,32,32]{6,3,2,5,1,4,0:T(8,128)S(1)} fusion(f32[]{:T(128)} %bitcast.9, f32[4,16,64,1,1,1,1]{2,1,6,5,4,3,0:T(8,128)S(1)} %bitcast.157, f32[2,2,32,2,32,64,1]{5,4,3,2,1,0,6:T(8,128)} %bitcast.151), kind=kOutput, calls=%fused_computation.3 | convolution fusion | flops 403177472 | bytes 4210692 | tf_op jit(solution)/shard_map/gja,gabm->gjbm/dot_general | solution.py:136
  144.0 8.0 %copy.55 = f32[4,2,2,16,2,32,32]{6,5,4,3,2,1,0:T(8,128)} copy(f32[4,2,2,16,2,32,32]{6,3,2,5,1,4,0:T(8,128)S(1)} %multiply_bitcast_fusion) | data formatting | bytes 4194304 | tf_op jit(solution)/shard_map/transpose | solution.py:149
  152.0 6.1 %reshape.194 = f32[16,32768]{1,0:T(8,128)S(1)} reshape(f32[4,2,2,16,2,32,32]{6,5,4,3,2,1,0:T(8,128)} %copy.55) | data formatting | bytes 4194304 | tf_op jit(solution)/shard_map/reshape | solution.py:150
  164.8 134.0 %all-reduce.2.cloned.1.call-done = f32[16,32768]{1,0:T(8,128)} async-done(((f32[16,32768]{1,0:T(8,128)}), f32[16,32768]{1,0:T(8,128)}) %all-reduce.2.cloned.1.call-update) | async-done | bytes 2097168 | tf_op jit(solution)/shard_map/psum | solution.py:102
  301.9 4.4 scatter_custom_fusion
  306.2 4.8 %reshape.195 = f32[4,2,2,16,2,32,32]{6,5,4,3,2,1,0:T(8,128)} reshape(f32[16,32768]{1,0:T(8,128)S(1)} %scatter_custom_fusion) | data formatting | bytes 4194304 | tf_op jit(solution)/shard_map/reshape | solution.py:154
  311.0 15.4 %copy.56 = f32[4,16,2,2,32,2,32]{6,5,4,3,1,0,2:T(2,128)} copy(f32[4,16,2,2,32,2,32]{6,4,2,1,5,3,0:T(8,128)} %bitcast.150) | data formatting | bytes 4194304 | tf_op jit(solution)/shard_map/transpose | solution.py:155
  326.4 12.2 %reshape.196 = f32[64,2,4096]{2,0,1:T(8,128)S(1)} reshape(f32[4,16,2,2,32,2,32]{6,5,4,3,1,0,2:T(2,128)} %copy.56) | data formatting | bytes 4194304 | tf_op jit(solution)/shard_map/reshape | solution.py:156
  343.4 20.4 %all-to-all-start.1 = ((f32[1,64,2,4096]{3,2,0,1:T(2,128)}), f32[1,64,2,4096]{3,2,0,1:T(2,128)S(1)}, u32[]{:S(2)}, u32[]{:S(2)}) async-start(f32[1,64,2,4096]{3,2,0,1:T(2,128)} %copy.57), calls=%async_computation.1 | async-start | bytes 4194304 | tf_op jit(solution)/shard_map/all_to_all | solution.py:159
  364.6 49.2 %all-to-all-done.1 = f32[1,64,2,4096]{3,2,0,1:T(2,128)S(1)} async-done(((f32[1,64,2,4096]{3,2,0,1:T(2,128)}), f32[1,64,2,4096]{3,2,0,1:T(2,128)S(1)}, u32[]{:S(2)}, u32[]{:S(2)}) %all-to-all-start.1) | async-done | bytes 2097184 | tf_op jit(solution)/shard_map/all_to_all | solution.py:159
  415.2 3.7 reshape.197
  419.0 3.6 convolution_bitcast_fusion
  425.5 8.6 %fusion.29 = f32[2,64,64,64]{3,2,1,0:T(8,128)S(1)} fusion(f32[2,64,64,64]{3,2,1,0:T(8,128)} %reshape.198, f32[64,64,1,1]{1,0,3,2:T(8,128)S(1)} %bitcast.159), kind=kOutput, calls=%fused_computation.66 | convolution fusion | flops 402653184 | bytes 4210688 | tf_op jit(solution)/shard_map/gjc,gabcl->gabjl/dot_general | solution.py:162
  434.2 8.4 %fusion = f32[2,64,64,64]{3,2,1,0:T(8,128)} fusion(f32[64,64,1,1]{1,0,3,2:T(8,128)S(1)} %bitcast.158, f32[2,64,64,64]{3,2,1,0:T(8,128)S(1)} %fusion.29), kind=kOutput, calls=%fused_computation.7 | convolution fusion | flops 402653184 | bytes 4210688 | tf_op jit(solution)/shard_map/gjl,gabcl->gabcj/dot_general | solution.py:163
  442.6 4.8 %reshape.200 = f32[1,2,64,4096]{3,2,1,0:T(8,128)} reshape(f32[2,64,64,64]{3,2,1,0:T(8,128)} %fusion) | data formatting | bytes 4194304 | tf_op jit(solution)/shard_map/reshape | solution.py:164
  (60 shorter events, 32.1 us)
Async XLA Ops:
  7.8 5.9 %copy-start.8 = (f32[2,64,64]{2,0,1:T(2,128)S(1)}, f32[2,64,64]{2,0,1:T(2,128)}, u32[]{:S(2)}) copy-start(f32[2,64,64]{2,0,1:T(2,128)} %constant.140) | copy-start | bytes 98308
  48.2 14.7 %copy-start.3 = (s32[16,4]{0,1:T(4,128)S(1)}, s32[16,4]{0,1:T(4,128)}, u32[]{:S(2)}) copy-start(s32[16,4]{0,1:T(4,128)} %param.14) | copy-start | bytes 772
  48.2 14.8 %copy-start.4 = (s32[16,4]{0,1:T(4,128)S(1)}, s32[16,4]{0,1:T(4,128)}, u32[]{:S(2)}) copy-start(s32[16,4]{0,1:T(4,128)} %constant.129.clone) | copy-start | bytes 772
  48.2 15.4 %copy-start.6 = (s32[16]{0:T(128)S(1)}, s32[16]{0:T(128)}, u32[]{:S(2)}) copy-start(s32[16]{0:T(128)} %constant.130.clone) | copy-start | bytes 196
  48.2 16.2 %copy-start.5 = (s32[4]{0:T(128)S(1)}, s32[4]{0:T(128)}, u32[]{:S(2)}) copy-start(s32[4]{0:T(128)} %constant.137) | copy-start | bytes 52
  48.2 18.9 %copy-start.2 = (f32[3,64,64]{2,0,1:T(4,128)S(1)}, f32[3,64,64]{2,0,1:T(4,128)}, u32[]{:S(2)}) copy-start(f32[3,64,64]{2,0,1:T(4,128)} %constant.139) | copy-start | bytes 147460
  48.3 64.7 %all-to-all-start = ((f32[1,2,64,4096]{3,1,0,2:T(2,128)}), f32[1,2,64,4096]{3,1,0,2:T(2,128)S(1)}, u32[]{:S(2)}, u32[]{:S(2)}) async-start(f32[1,2,64,4096]{3,1,0,2:T(2,128)} %copy.52), calls=%async_computation | async-start | bytes 4194304 | tf_op jit(solution)/shard_map/all_to_all | solution.py:139
  62.8 235.9 %all-reduce.2.cloned.1.call-start = ((), (), s32[]{:S(2)}) async-start(), calls=%async_computation.2 | async-start | bytes 4194304 | tf_op jit(solution)/shard_map/psum | solution.py:102
  112.9 1.3 copy-start
  163.6 0.9 copy-start.1
  343.4 20.4 %copy-start.7 = (f32[2,64,64]{2,0,1:T(2,128)S(1)}, f32[2,64,64]{2,0,1:T(2,128)}, u32[]{:S(2)}) copy-start(f32[2,64,64]{2,0,1:T(2,128)} %constant.141) | copy-start | bytes 98308
  343.4 70.3 %all-to-all-start.1 = ((f32[1,64,2,4096]{3,2,0,1:T(2,128)}), f32[1,64,2,4096]{3,2,0,1:T(2,128)S(1)}, u32[]{:S(2)}, u32[]{:S(2)}) async-start(f32[1,64,2,4096]{3,2,0,1:T(2,128)} %copy.57), calls=%async_computation.1 | async-start | bytes 4194304 | tf_op jit(solution)/shard_map/all_to_all | solution.py:159
Sparse Core Ops, SparseCore 0:
  163.8 134.9 all-reduce.1
where the time goes:
time: 461 us; the launch traced here: 455 us
  waiting for transfers between devices  229 us (50%)
  local copies, waits for them, and re-layouts  93.4 us (20%)
  matrix products  68.2 us (15%)
  starting transfers between devices  35 us (8%)
  between operations  16.5 us (4%)
  other arithmetic  12.8 us (3%)
    psum x1, waiting for transfers between devices, combine(): summed = lax.psum(pick_rows(blocks, order, valid), ('half', 'grid'))  134 us
    all_to_all x1, waiting for transfers between devices, per_device(): lax.all_to_all(expanded, 'dom', split_axis=1, concat_axis=2, tiled=True)  49.2 us
    all_to_all x1, waiting for transfers between devices, per_device(): lax.all_to_all(values, 'dom', split_axis=2, concat_axis=1, tiled=True)  45.5 us
    dot_general x1, matrix products, per_device(): jnp.einsum('gja,gabm->gjbm', forward_mats[0], lax.all_to_all(values, 'dom...  22.9 us
    all_to_all x1, starting transfers between devices, per_device(): lax.all_to_all(expanded, 'dom', split_axis=1, concat_axis=2, tiled=True)  20.4 us
    transpose x1, local copies, waits for them, and re-layouts, per_device(): totals = summed_blocks.reshape(4, 2, 2, quarter_rows, pole_rows, N3 // 2,...  15.4 us
    another operation x4, local copies, waits for them, and re-layouts  15.1 us
    all_to_all x1, starting transfers between devices, per_device(): lax.all_to_all(values, 'dom', split_axis=2, concat_axis=1, tiled=True)  14.6 us
  transfers between devices with their start and end apart: 3, of which 3 were waited for; matrix products, arithmetic and copies ran while one was open for 1% of the time, Pallas kernels for 0%

commit v1 on v0

--- a/solution.py
+++ b/solution.py
@@ -14,6 +14,12 @@
 N4 = 64
 HIGH = lax.Precision.HIGHEST
 SPANS = (2, 1, 1, 1)
+
+
+def gather_and_add(array, name):
+    parts = lax.all_gather(array, name, axis=0, tiled=False)
+    total = parts.sum(axis=0)
+    return total
 
 
 def level_ordering(level):
@@ -99,7 +105,7 @@
 
 def combine(blocks, covered):
     order, valid = compact_order(jnp.any(covered, axis=0))
-    summed = lax.psum(pick_rows(blocks, order, valid), ("half", "grid"))
+    summed = gather_and_add(pick_rows(blocks, order, valid), ("half", "grid"))
     return place_rows(summed, order, valid)
 
 

time: 461 us -> 681 us (1.48)
  waiting for transfers between devices: 229 us -> 447 us
  other arithmetic: 12.8 us -> 23 us
  starting transfers between devices: 35 us -> 25.4 us
    all_gather x0 -> x1, waiting for transfers between devices: none -> 352 us  [gather_and_add(): parts = lax.all_gather(array, name, axis=0, tiled=False)]
    psum x1 -> x0, waiting for transfers between devices: 134 us -> none  [combine(): summed = lax.psum(pick_rows(blocks, order, valid), ('half', 'grid'))]
    reduce_sum x0 -> x1, other arithmetic: none -> 11.7 us  [gather_and_add(): total = parts.sum(axis=0)]
    all_to_all x1, starting transfers between devices: 20.4 us -> 10.8 us  [per_device(): lax.all_to_all(expanded, 'dom', split_axis=1, concat_axis=2, tiled=True)]
where the time goes in v1:
time: 681 us; the launch traced here: 674 us
  waiting for transfers between devices  447 us (66%)
  local copies, waits for them, and re-layouts  93.4 us (14%)
  matrix products  68.2 us (10%)
  starting transfers between devices  25.4 us (4%)
  other arithmetic  23 us (3%)
  between operations  16.5 us (2%)
    all_gather x1, waiting for transfers between devices, gather_and_add(): parts = lax.all_gather(array, name, axis=0, tiled=False)  352 us
    all_to_all x1, waiting for transfers between devices, per_device(): lax.all_to_all(expanded, 'dom', split_axis=1, concat_axis=2, tiled=True)  49.2 us
    all_to_all x1, waiting for transfers between devices, per_device(): lax.all_to_all(values, 'dom', split_axis=2, concat_axis=1, tiled=True)  45.5 us
    dot_general x1, matrix products, per_device(): jnp.einsum('gja,gabm->gjbm', forward_mats[0], lax.all_to_all(values, 'dom...  22.9 us
    transpose x1, local copies, waits for them, and re-layouts, per_device(): totals = summed_blocks.reshape(4, 2, 2, quarter_rows, pole_rows, N3 // 2,...  15.4 us
    another operation x4, local copies, waits for them, and re-layouts  15.1 us
    all_to_all x1, starting transfers between devices, per_device(): lax.all_to_all(values, 'dom', split_axis=2, concat_axis=1, tiled=True)  14.6 us
    dot_general x1, matrix products, per_device(): jnp.einsum('gjl,gabcl->gabcj', forward_mats[3], values, precision=HIGH)  13.8 us
  transfers between devices with their start and end apart: 3, of which 3 were waited for; matrix products, arithmetic and copies ran while one was open for 1% of the time, Pallas kernels for 0%

profile of v1, /device:TPU:1, one launch (start us, length us, event | category | flops | bytes accessed | tf_op | source)
XLA Modules:
  0.0 673.6 jit_solution(6602590551772174916)
XLA Ops:
  7.8 4.6 reshape.237
  14.2 13.8 %fusion.29 = f32[64,2,64,64]{3,0,2,1:T(8,128)S(1)} fusion(f32[64,64,1,1]{1,0,3,2:T(8,128)S(1)} %bitcast.166, f32[2,64,64,64]{3,2,1,0:T(8,128)} %reshape.237), kind=kOutput, calls=%fused_computation.66 | convolution fusion | flops 402653184 | bytes 4210688 | tf_op jit(solution)/shard_map/gjl,gabcl->gabcj/dot_general | solution.py:134
  28.0 4.9 fusion.4
  33.0 5.7 copy.51
  38.6 3.7 reshape.238
  48.3 14.6 %all-to-all-start = ((f32[1,2,64,4096]{3,1,0,2:T(2,128)}), f32[1,2,64,4096]{3,1,0,2:T(2,128)S(1)}, u32[]{:S(2)}, u32[]{:S(2)}) async-start(f32[1,2,64,4096]{3,1,0,2:T(2,128)} %copy.52), calls=%async_computation | async-start | bytes 4194304 | tf_op jit(solution)/shard_map/all_to_all | solution.py:145
  67.4 45.5 %all-to-all-done = f32[1,2,64,4096]{3,1,0,2:T(2,128)S(1)} async-done(((f32[1,2,64,4096]{3,1,0,2:T(2,128)}), f32[1,2,64,4096]{3,1,0,2:T(2,128)S(1)}, u32[]{:S(2)}, u32[]{:S(2)}) %all-to-all-start) | async-done | bytes 2097184 | tf_op jit(solution)/shard_map/all_to_all | solution.py:145
  117.5 3.6 copy.54
  121.1 22.9 %multiply_bitcast_fusion = f32[4,2,2,16,2,32,32]{6,3,2,5,1,4,0:T(8,128)S(1)} fusion(f32[]{:T(128)} %bitcast.9, f32[4,16,64,1,1,1,1]{2,1,6,5,4,3,0:T(8,128)S(1)} %bitcast.161, f32[2,2,32,2,32,64,1]{5,4,3,2,1,0,6:T(8,128)} %bitcast.155), kind=kOutput, calls=%fused_computation.3 | convolution fusion | flops 403177472 | bytes 4210692 | tf_op jit(solution)/shard_map/gja,gabm->gjbm/dot_general | solution.py:142
  144.0 8.0 %copy.55 = f32[4,2,2,16,2,32,32]{6,5,4,3,2,1,0:T(8,128)} copy(f32[4,2,2,16,2,32,32]{6,3,2,5,1,4,0:T(8,128)S(1)} %multiply_bitcast_fusion) | data formatting | bytes 4194304 | tf_op jit(solution)/shard_map/transpose | solution.py:155
  152.0 6.1 reshape.240
  164.8 352.5 %all-gather.2.cloned.1.call-done = f32[16,16,32768]{2,1,0:T(8,128)} async-done(((f32[1,16,32768]{2,1,0:T(8,128)}), f32[16,16,32768]{2,1,0:T(8,128)}) %all-gather.2.cloned.1.call-update) | async-done | bytes 33554448 | tf_op jit(solution)/shard_map/all_gather | solution.py:20
  517.3 11.7 %reduce_sum.19 = f32[16,32768]{1,0:T(8,128)S(1)} reduce(f32[16,16,32768]{2,1,0:T(8,128)} %all-gather.2.cloned.1.call-done, f32[]{:T(128)} %constant.117.clone.1), dimensions={0}, to_apply=%region_5.6 | reduce | flops 7864320 | bytes 35651588 | tf_op jit(solution)/shard_map/reduce_sum | solution.py:21
  530.5 4.4 scatter_custom_fusion
  534.9 4.8 reshape.241
  539.7 15.4 %copy.56 = f32[4,16,2,2,32,2,32]{6,5,4,3,1,0,2:T(2,128)} copy(f32[4,16,2,2,32,2,32]{6,4,2,1,5,3,0:T(8,128)} %bitcast.154) | data formatting | bytes 4194304 | tf_op jit(solution)/shard_map/transpose | solution.py:161
  555.1 12.2 %reshape.242 = f32[64,2,4096]{2,0,1:T(8,128)S(1)} reshape(f32[4,16,2,2,32,2,32]{6,5,4,3,1,0,2:T(2,128)} %copy.56) | data formatting | bytes 4194304 | tf_op jit(solution)/shard_map/reshape | solution.py:162
  572.1 10.8 %all-to-all-start.1 = ((f32[1,64,2,4096]{3,2,0,1:T(2,128)}), f32[1,64,2,4096]{3,2,0,1:T(2,128)S(1)}, u32[]{:S(2)}, u32[]{:S(2)}) async-start(f32[1,64,2,4096]{3,2,0,1:T(2,128)} %copy.57), calls=%async_computation.1 | async-start | bytes 4194304 | tf_op jit(solution)/shard_map/all_to_all | solution.py:165
  583.7 49.2 %all-to-all-done.1 = f32[1,64,2,4096]{3,2,0,1:T(2,128)S(1)} async-done(((f32[1,64,2,4096]{3,2,0,1:T(2,128)}), f32[1,64,2,4096]{3,2,0,1:T(2,128)S(1)}, u32[]{:S(2)}, u32[]{:S(2)}) %all-to-all-start.1) | async-done | bytes 2097184 | tf_op jit(solution)/shard_map/all_to_all | solution.py:165
  634.3 3.7 reshape.243
  638.0 3.6 convolution_bitcast_fusion
  644.6 8.6 %fusion.30 = f32[2,64,64,64]{3,2,1,0:T(8,128)S(1)} fusion(f32[2,64,64,64]{3,2,1,0:T(8,128)} %reshape.244, f32[64,64,1,1]{1,0,3,2:T(8,128)S(1)} %bitcast.163), kind=kOutput, calls=%fused_computation.67 | convolution fusion | flops 402653184 | bytes 4210688 | tf_op jit(solution)/shard_map/gjc,gabcl->gabjl/dot_general | solution.py:168
  653.3 8.4 %fusion = f32[2,64,64,64]{3,2,1,0:T(8,128)} fusion(f32[64,64,1,1]{1,0,3,2:T(8,128)S(1)} %bitcast.162, f32[2,64,64,64]{3,2,1,0:T(8,128)S(1)} %fusion.30), kind=kOutput, calls=%fused_computation.7 | convolution fusion | flops 402653184 | bytes 4210688 | tf_op jit(solution)/shard_map/gjl,gabcl->gabcj/dot_general | solution.py:169
  661.6 4.8 reshape.246
  (61 shorter events, 33.7 us)
Async XLA Ops:
  7.8 5.9 copy-start.8
  48.2 14.7 %copy-start.3 = (s32[16,4]{0,1:T(4,128)S(1)}, s32[16,4]{0,1:T(4,128)}, u32[]{:S(2)}) copy-start(s32[16,4]{0,1:T(4,128)} %param.14) | copy-start | bytes 772
  48.2 14.8 %copy-start.4 = (s32[16,4]{0,1:T(4,128)S(1)}, s32[16,4]{0,1:T(4,128)}, u32[]{:S(2)}) copy-start(s32[16,4]{0,1:T(4,128)} %constant.130.clone) | copy-start | bytes 772
  48.2 15.4 %copy-start.6 = (s32[16]{0:T(128)S(1)}, s32[16]{0:T(128)}, u32[]{:S(2)}) copy-start(s32[16]{0:T(128)} %constant.131.clone) | copy-start | bytes 196
  48.2 16.2 %copy-start.5 = (s32[4]{0:T(128)S(1)}, s32[4]{0:T(128)}, u32[]{:S(2)}) copy-start(s32[4]{0:T(128)} %constant.138) | copy-start | bytes 52
  48.2 18.9 %copy-start.2 = (f32[3,64,64]{2,0,1:T(4,128)S(1)}, f32[3,64,64]{2,0,1:T(4,128)}, u32[]{:S(2)}) copy-start(f32[3,64,64]{2,0,1:T(4,128)} %constant.140) | copy-start | bytes 147460
  48.3 64.7 %all-to-all-start = ((f32[1,2,64,4096]{3,1,0,2:T(2,128)}), f32[1,2,64,4096]{3,1,0,2:T(2,128)S(1)}, u32[]{:S(2)}, u32[]{:S(2)}) async-start(f32[1,2,64,4096]{3,1,0,2:T(2,128)} %copy.52), calls=%async_computation | async-start | bytes 4194304 | tf_op jit(solution)/shard_map/all_to_all | solution.py:145
  62.8 454.5 %all-gather.2.cloned.1.call-start = ((), (), s32[]{:S(2)}) async-start(), calls=%async_computation.2 | async-start | bytes 35651584 | tf_op jit(solution)/shard_map/all_gather | solution.py:20
  112.9 1.3 copy-start
  163.6 0.9 copy-start.1
  572.1 10.8 %copy-start.7 = (f32[2,64,64]{2,0,1:T(2,128)S(1)}, f32[2,64,64]{2,0,1:T(2,128)}, u32[]{:S(2)}) copy-start(f32[2,64,64]{2,0,1:T(2,128)} %constant.142) | copy-start | bytes 98308
  572.1 60.7 %all-to-all-start.1 = ((f32[1,64,2,4096]{3,2,0,1:T(2,128)}), f32[1,64,2,4096]{3,2,0,1:T(2,128)S(1)}, u32[]{:S(2)}, u32[]{:S(2)}) async-start(f32[1,64,2,4096]{3,2,0,1:T(2,128)} %copy.57), calls=%async_computation.1 | async-start | bytes 4194304 | tf_op jit(solution)/shard_map/all_to_all | solution.py:165
Sparse Core Ops, SparseCore 0:
  163.8 353.4 all-gather.1
